TPU v7x, 32 devices: a whole 2x2x4 slice. The times are simulated.
32 devices in a mesh: group: 2 (over x), tok: 16 (over z, y, core).
Axes of the slice: x: 2, y: 2, z: 4, core: 2. Of those that a mesh axis runs over, the one named last changes fastest.
Arguments:
- hidden: bfloat16 [4096, 6144], P(('group', 'tok')), parts along dimension 0, may hold values from -6 to 6
- ln_gain: bfloat16 [6144], replicated, may hold values from 0.099609375 to 1.8984375
- router: bfloat16 [6144, 16], replicated, may hold values from -0.078125 to 0.078125
- routes: int32 [4096, 4], P(('group', 'tok')), parts along dimension 0, may hold values from 0 to 15, as said below
- w_gate: bfloat16 [16, 6144, 128], P('tok'), may hold values from -0.078125 to 0.078125
- w_up: bfloat16 [16, 6144, 128], P('tok'), may hold values from -0.078125 to 0.078125
- w_down: bfloat16 [16, 128, 6144], P('tok'), may hold values from -0.25 to 0.25
Outputs:
- mixed: bfloat16 [4096, 6144], P(('group', 'tok')), parts along dimension 0
There are 2 independent parts, one for each index of `group`. A program takes and returns all parts, laid end to end along the dimension named above; an argument that names none is the same for every part. Nothing has to cross between parts.
Inputs may be any that keep to these rules, and one draw needn't show every extreme that they name: `routes`: the 4 experts of a row differ. In each aligned block of 64 rows (one micro-batch of one device) each served expert 0 to 1 is named by 1 to 4 rows, and one served expert, the same in all blocks of a part, by exactly 4; experts 2 and above have no such bound.
All inputs are finite; a program needn't handle non-finite values.
Results may differ from a plain program's by a relative error of at most 0.0026.
Values may be sent and summed in bfloat16 or wider, within the bound.
A program may use at most 128 MiB of HBM per device.

v0:
```python
import jax
import jax.numpy as jnp
from jax import lax
from jax.sharding import PartitionSpec as P

EXPERTS = 16
TOP = 4
EXP_WIN = 2
MB_ROWS = 64
MB_DEV = 2
MOST = 4


EPS = 1e-05


def layer_norm(hidden, ln_gain):
    values = hidden.astype(jnp.float32)
    center = jnp.mean(values, axis=-1, keepdims=True)
    spread = jnp.mean(jnp.square(values - center), axis=-1, keepdims=True)
    return ((values - center) * lax.rsqrt(spread + EPS) * ln_gain.astype(jnp.float32)).astype(
        jnp.bfloat16
    )


def gate_values(normed, router, routes):
    logits = jnp.dot(normed, router, preferred_element_type=jnp.float32)
    onehot = routes[:, :, None] == jnp.arange(EXPERTS, dtype=jnp.int32)[None, None, :]
    chosen = jnp.sum(jnp.where(onehot, logits[:, None, :], jnp.zeros((), jnp.float32)), axis=-1)
    raised = jnp.exp(chosen)
    return (raised / jnp.sum(raised, axis=-1, keepdims=True), onehot)


def placement(onehot, routes, blocks, block_rows):
    pair_hot = onehot.reshape(blocks, block_rows * TOP, EXPERTS).astype(jnp.int32)
    earlier = jnp.cumsum(pair_hot, axis=1) - pair_hot
    placed = jnp.sum(earlier * pair_hot, axis=-1)
    expert_ids = routes.reshape(blocks, block_rows * TOP)
    return (expert_ids, placed)


def gather_rows(normed, slot_table):
    filled = slot_table >= 0
    picked = jnp.take(normed, jnp.maximum(slot_table, 0), axis=0)
    return jnp.where(filled[:, None], picked, jnp.zeros((), normed.dtype))


def expert_block(slot_block, w_gate, w_up, w_down):
    send_rows = slot_block.reshape(-1, slot_block.shape[-1])
    gate_out = jnp.dot(send_rows, w_gate[0], preferred_element_type=jnp.float32)
    up_out = jnp.dot(send_rows, w_up[0], preferred_element_type=jnp.float32)
    hidden_act = (jax.nn.silu(gate_out) * up_out).astype(jnp.bfloat16)
    out_rows = jnp.dot(hidden_act, w_down[0], preferred_element_type=jnp.float32).astype(
        jnp.bfloat16
    )
    return out_rows.reshape(slot_block.shape)


def route_block(send_block, w_gate, w_up, w_down):
    return lax.all_to_all(
        expert_block(
            lax.all_to_all(send_block, "tok", split_axis=0, concat_axis=0, tiled=True),
            w_gate,
            w_up,
            w_down,
        ),
        "tok",
        split_axis=0,
        concat_axis=0,
        tiled=True,
    )


def send_rows_for(normed, slot_flat, token_ids, slot_count, windows):
    slot_table = (
        jnp.full((EXP_WIN * slot_count,), -1, jnp.int32).at[slot_flat].set(token_ids, mode="drop")
    )
    rows = gather_rows(normed, slot_table).reshape(EXP_WIN, 1, slot_count, normed.shape[1])
    spread_rows = jnp.broadcast_to(rows, (EXP_WIN, windows, slot_count, normed.shape[1]))
    return spread_rows.reshape(EXP_WIN * windows, slot_count, normed.shape[1])


def combine_rows(returned, slot_flat, gate_flat, served, hidden, slot_count, windows):
    model_width = hidden.shape[1]
    expert_sum = jnp.sum(
        returned.reshape(EXP_WIN, windows, slot_count, model_width), axis=1, dtype=jnp.float32
    )
    expert_sum = expert_sum.reshape(EXP_WIN * slot_count, model_width)
    safe_index = jnp.where(served, slot_flat, 0)
    picked = jnp.take(expert_sum, safe_index, axis=0).reshape(hidden.shape[0], TOP, model_width)
    gate_used = jnp.where(served, gate_flat, jnp.zeros((), jnp.float32)).reshape(-1, TOP)
    weighted = jnp.einsum("tk,tkd->td", gate_used, picked)
    return (hidden.astype(jnp.float32) + weighted).astype(jnp.bfloat16)


def body(hidden, ln_gain, router, routes, w_gate, w_up, w_down):
    devices = lax.axis_size("tok")
    windows = devices // EXP_WIN
    block_rows = MB_ROWS
    micro_count = MB_DEV
    most_rows = MOST
    normed = layer_norm(hidden, ln_gain)
    gates, onehot = gate_values(normed, router, routes)
    expert_ids, placed = placement(onehot, routes, micro_count, block_rows)
    served = expert_ids < EXP_WIN
    micro_ids = jnp.arange(micro_count, dtype=jnp.int32)[:, None]
    token_ids = (
        micro_ids * block_rows + jnp.arange(block_rows * TOP, dtype=jnp.int32)[None, :] // TOP
    )
    gate_flat = gates.reshape(micro_count, block_rows * TOP)
    slot_count = micro_count * most_rows
    slot = micro_ids * most_rows + placed
    slot_flat = jnp.where(served, expert_ids * slot_count + slot, EXP_WIN * slot_count).reshape(-1)
    send_block = send_rows_for(normed, slot_flat, token_ids.reshape(-1), slot_count, windows)
    returned = route_block(send_block, w_gate, w_up, w_down)
    return combine_rows(
        returned, slot_flat, gate_flat.reshape(-1), served.reshape(-1), hidden, slot_count, windows
    )


def solution(mesh):
    in_specs = (
        P(("group", "tok"), None),
        P(),
        P(),
        P(("group", "tok"), None),
        P("tok", None, None),
        P("tok", None, None),
        P("tok", None, None),
    )
    out_specs = P(("group", "tok"), None)
    return jax.shard_map(body, mesh=mesh, in_specs=in_specs, out_specs=out_specs, check_vma=False)
```

profile of v0, /device:TPU:15, one launch (start us, length us, event | category | flops | bytes accessed | tf_op | source)
XLA Modules:
  0.0 135.6 jit_solution(4913659478285619753)
XLA Ops:
  0.0 0.9 copy.18
  1.2 0.7 broadcast_multiply_fusion
  1.9 1.2 reduce-window.6
  3.0 0.2 slice_reduce_fusion
  3.8 0.7 compare_and_fusion
  5.1 2.4 %scatter_custom_fusion = s32[16]{0:T(128)S(1)} fusion(s32[512]{0:T(512)S(1)} %bitcast.77, s32[512]{0:T(512)S(1)} %bitcast.78, s32[]{:T(128)} %constant.70.clone.1), kind=kCustom, calls=%fused_computation.72 | custom fusion | bytes 68 | tf_op jit(solution)/shard_map/scatter | solution.py:76
  7.6 0.7 convert_element_type.33
  8.3 1.7 %convert_reduce_fusion = f32[128]{0:T(128)S(1)} fusion(bf16[128,6144]{1,0:T(8,128)(2,1)} %param.7), kind=kLoop, calls=%fused_computation.11 | loop fusion | flops 1572736 | bytes 1573376 | tf_op jit(solution)/shard_map/reduce_sum | solution.py:19
  10.0 0.6 fusion.7
  10.8 1.7 %fusion.9 = bf16[128,6144]{1,0:T(8,128)(2,1)} fusion(bf16[128,6144]{1,0:T(8,128)(2,1)S(1)} %copy-done.1, f32[6144]{0:T(1024)S(1)} %convert_element_type.33, f32[128]{0:T(128)S(1)} %add_rsqrt_fusion, f32[128]{0:T(128)S(1)} %broadcast_multiply_fusion.1), kind=kLoop, calls=%fused_computation.16 | loop fusion | flops 3932160 | bytes 3171328 | tf_op jit(solution)/shard_map/convert_element_type | solution.py:21
  12.4 2.5 %gather_fusion = bf16[16,6144]{1,0:T(8,128)(2,1)S(1)} fusion(bf16[128,6144]{1,0:T(8,128)(2,1)} %fusion.9, s32[1024]{0:T(1024)S(1)} %pad_clamp_fusion.1), kind=kCustom, calls=%fused_computation | custom fusion | bytes 393280 | tf_op jit(solution)/shard_map/jit(_take)/gather | solution.py:44
  15.0 0.1 broadcast_in_dim.97
  15.2 42.6 %all_to_all.10 = bf16[16,8,6144]{2,1,0:T(8,128)(2,1)S(1)} all-to-all(bf16[16,8,6144]{2,1,0:T(8,128)(2,1)S(1)} %bitcast.74), channel_id=1, replica_groups=mesh['group'=2,'tok'=16] {'tok'}, dimensions={0} | all-to-all | bytes 3145728 | tf_op jit(solution)/shard_map/all_to_all | solution.py:62
  57.7 1.1 copy-done.2
  58.9 0.6 fusion.14
  59.5 4.1 %fusion.2 = bf16[16,8,6144]{2,1,0:T(8,128)(2,1)} fusion(bf16[1,128,6144]{2,1,0:T(8,128)(2,1)S(1)} %copy-done, bf16[1,6144,128]{2,1,0:T(8,128)(2,1)} %param.12, bf16[16,8,6144]{2,1,0:T(8,128)(2,1)} %copy-done.2, f32[128,128]{1,0:T(8,128)S(1)} %fusion.14), kind=kOutput, calls=%fused_computation.6 | convolution fusion | flops 403537920 | bytes 6356992 | tf_op jit(solution)/shard_map/dot_general | solution.py:53
  63.6 5.2 %all-to-all-start.1 = ((bf16[16,8,6144]{2,1,0:T(8,128)(2,1)}), bf16[16,8,6144]{2,1,0:T(8,128)(2,1)}, u32[]{:S(2)}, u32[]{:S(2)}) async-start(bf16[16,8,6144]{2,1,0:T(8,128)(2,1)} %fusion.2), calls=%async_computation.1 | async-start | bytes 3145728 | tf_op jit(solution)/shard_map/all_to_all | solution.py:60
  68.8 1.9 %fusion.48 = f32[128,16]{0,1:T(8,128)S(1)} fusion(bf16[128,6144]{1,0:T(8,128)(2,1)} %fusion.9, bf16[6144,16]{0,1:T(8,128)(2,1)S(1)} %copy-done.4), kind=kOutput, calls=%fused_computation.77 | convolution fusion | flops 25165824 | bytes 1777664 | tf_op jit(solution)/shard_map/dot_general | solution.py:27
  71.1 34.0 %all-to-all-done.1 = bf16[16,8,6144]{2,1,0:T(8,128)(2,1)} async-done(((bf16[16,8,6144]{2,1,0:T(8,128)(2,1)}), bf16[16,8,6144]{2,1,0:T(8,128)(2,1)}, u32[]{:S(2)}, u32[]{:S(2)}) %all-to-all-start.1) | async-done | bytes 1572896 | tf_op jit(solution)/shard_map/all_to_all | solution.py:60
  105.0 1.6 %convert_reduce_fusion.1 = bf16[2,8,6144]{2,1,0:T(8,128)(2,1)S(1)} fusion(bf16[16,8,6144]{2,1,0:T(8,128)(2,1)} %all-to-all-done.1), kind=kLoop, calls=%fused_computation.18 | loop fusion | flops 1474560 | bytes 1769472 | tf_op jit(solution)/shard_map/reduce_sum | solution.py:85
  106.7 6.0 %gather_fusion.1 = bf16[512,6144]{1,0:T(8,128)(2,1)} fusion(bf16[16,6144]{1,0:T(8,128)(2,1)S(1)} %bitcast.73, s32[1024]{0:T(1024)S(1)} %pad_clamp_fusion), kind=kCustom, calls=%fused_computation.1 | custom fusion | bytes 12584960 | tf_op jit(solution)/shard_map/jit(_take)/gather | solution.py:90
  112.7 10.9 %gather.15 = bf16[128,4,6144]{2,1,0:T(4,128)(2,1)} reshape(bf16[512,6144]{1,0:T(8,128)(2,1)} %gather_fusion.1) | data formatting | bytes 12582912 | tf_op jit(solution)/shard_map/jit(_take)/gather | solution.py:90
  123.6 8.0 %fusion = f32[128,1,6144]{2,1,0:T(1,128)} fusion(bf16[128,4,1]{1,2,0:T(2,128)(2,1)S(1)} %copy.25, bf16[128,4,6144]{2,1,0:T(4,128)(2,1)} %gather.15, pred[128,4]{1,0:T(8,128)(4,1)S(1)} %copy.22), kind=kOutput, calls=%fused_computation.3 | convolution fusion | flops 9437184 | bytes 9438720 | tf_op jit(solution)/shard_map/tk,tkd->td/dot_general | solution.py:92
  131.6 4.0 %fusion.10 = bf16[128,6144]{1,0:T(8,128)(2,1)} fusion(bf16[128,6144]{1,0:T(8,128)(2,1)S(1)} %copy-done.1, f32[128,1,6144]{2,1,0:T(1,128)} %fusion), kind=kLoop, calls=%fused_computation.17 | loop fusion | flops 2359296 | bytes 6291456 | tf_op jit(solution)/shard_map/convert_element_type | solution.py:93
  (47 shorter events, 2.0 us)
Async XLA Ops:
  0.0 59.4 %copy-start = (bf16[1,128,6144]{2,1,0:T(8,128)(2,1)S(1)}, bf16[1,128,6144]{2,1,0:T(8,128)(2,1)}, u32[]{:S(2)}) copy-start(bf16[1,128,6144]{2,1,0:T(8,128)(2,1)} %param.13) | copy-start | bytes 4718596
  0.0 10.0 %copy-start.1 = (bf16[128,6144]{1,0:T(8,128)(2,1)S(1)}, bf16[128,6144]{1,0:T(8,128)(2,1)}, u32[]{:S(2)}) copy-start(bf16[128,6144]{1,0:T(8,128)(2,1)} %param.7) | copy-start | bytes 4718596
  15.2 43.7 %copy-start.3 = (bf16[1,6144,128]{2,1,0:T(8,128)(2,1)S(1)}, bf16[1,6144,128]{2,1,0:T(8,128)(2,1)}, u32[]{:S(2)}) copy-start(bf16[1,6144,128]{2,1,0:T(8,128)(2,1)} %param.11) | copy-start | bytes 4718596
  57.7 1.1 copy-start.2
  63.6 5.2 %copy-start.4 = (bf16[6144,16]{0,1:T(8,128)(2,1)S(1)}, bf16[6144,16]{0,1:T(8,128)(2,1)}, u32[]{:S(2)}) copy-start(bf16[6144,16]{0,1:T(8,128)(2,1)} %param.9) | copy-start | bytes 589828
  63.6 41.5 %all-to-all-start.1 = ((bf16[16,8,6144]{2,1,0:T(8,128)(2,1)}), bf16[16,8,6144]{2,1,0:T(8,128)(2,1)}, u32[]{:S(2)}, u32[]{:S(2)}) async-start(bf16[16,8,6144]{2,1,0:T(8,128)(2,1)} %fusion.2), calls=%async_computation.1 | async-start | bytes 3145728 | tf_op jit(solution)/shard_map/all_to_all | solution.py:60
  68.8 1.9 %copy-start.5 = (s32[128,4]{0,1:T(4,128)S(1)}, s32[128,4]{0,1:T(4,128)}, u32[]{:S(2)}) copy-start(s32[128,4]{0,1:T(4,128)} %param.10) | copy-start | bytes 6148
where the time goes:
time: 136 us
  blocking collectives  42.6 us (31%)
  waiting for transfers between devices  34 us (25%)
  local copies, waits for them, and re-layouts  25.8 us (19%)
  matrix products  14.6 us (11%)
  other arithmetic  13.4 us (10%)
  starting transfers between devices  5.18 us (4%)
    all_to_all x1, blocking collectives, route_block(): lax.all_to_all(send_block, 'tok', split_axis=0, concat_axis=0, tiled=True)  42.6 us
    all_to_all x1, waiting for transfers between devices, route_block(): lax.all_to_all(expert_block(lax.all_to_all(send_block, 'tok', split_axis=...  34 us
    gather x2, local copies, waits for them, and re-layouts, combine_rows(): jnp.take(expert_sum, safe_index, axis=0)  16.9 us
    dot_general x1, matrix products, combine_rows(): weighted = jnp.einsum('tk,tkd->td', gate_used, picked)  7.98 us
    all_to_all x1, starting transfers between devices, route_block(): lax.all_to_all(expert_block(lax.all_to_all(send_block, 'tok', split_axis=...  5.18 us
    dot_general x1, matrix products, expert_block(): jnp.dot(hidden_act, w_down[0], preferred_element_type=jnp.float32)  4.11 us
    convert_element_type x1, other arithmetic, combine_rows(): return (hidden.astype(jnp.float32) + weighted).astype(jnp.bfloat16)  4.04 us
  transfers between devices with their start and end apart: 1, of which 1 were waited for; matrix products, arithmetic and copies ran while one was open for 2% of the time, Pallas kernels for 0%

commit v1 on v0

v1 whole, which is shorter than its diff:
```python
import functools

import jax
import jax.numpy as jnp
from jax import lax
from jax.experimental import pallas as pl
from jax.experimental.pallas import tpu as pltpu
from jax.sharding import PartitionSpec as P

EXPERTS = 16
TOP = 4
EXP_WIN = 2
MB_ROWS = 64
MB_DEV = 2
MOST = 4
SLOTS = MB_DEV * MOST

EPS = 1e-05
MESH = pl.DeviceIdType.MESH
F32 = jnp.float32
BF16 = jnp.bfloat16


def routes_plan(n):
    bits = n.bit_length() - 1
    inner = [1 << b for b in range(1, bits - 1)]
    half = n // 2
    orders = {0: inner[::-1], half: inner}

    def chain(slot):
        return half if slot & half else 0

    def later(slot):
        order = orders[chain(slot)]
        last = -1
        for at, bit in enumerate(order):
            if slot & bit:
                last = at
        return order[last + 1 :]

    def last_bit(slot):
        if slot & 1:
            return 1
        found = half
        for bit in orders[chain(slot)]:
            if slot & bit:
                found = bit
        return found

    evens = [slot for slot in range(n) if not slot & 1]

    def depth(slot):
        return bin(slot).count("1") + (1 if slot & half else 0)

    arrival = sorted([slot for slot in evens if slot], key=lambda slot: (depth(slot), slot & half))
    return later, last_bit, arrival


def kernel(n, hidden_hbm, gain_ref, router_hbm, routes_ref, wg_hbm, wu_hbm, wd_hbm, out_hbm,
           hidden, router, wg, wu, wd, x_buf, other, y_buf, z_buf, out,
           in_sem, out_sem, x_send, x_recv, z_send, z_recv):
    later, last_bit, arrival = routes_plan(n)
    half = n // 2
    tokens, width = hidden.shape
    cols = width // 2
    me = lax.axis_index("tok")

    def peer(bit):
        return {"tok": me + bit * (1 - 2 * lax.rem(lax.div(me, bit), 2))}

    load_hidden = pltpu.make_async_copy(hidden_hbm, hidden, in_sem.at[0])
    load_hidden.start()
    loads = [
        pltpu.make_async_copy(src, dst, in_sem.at[1 + at])
        for at, (src, dst) in enumerate(((router_hbm, router), (wg_hbm, wg), (wu_hbm, wu), (wd_hbm, wd)))
    ]
    for load in loads:
        load.start()

    barrier = pltpu.get_barrier_semaphore()
    bits = [1 << b for b in range(n.bit_length() - 1)]
    for bit in bits:
        pl.semaphore_signal(barrier, inc=1, device_id=peer(bit), device_id_type=MESH)

    my_expert = lax.div(me, half)
    token = lax.broadcasted_iota(jnp.int32, (2 * SLOTS, tokens), 1)
    slot_at = lax.broadcasted_iota(jnp.int32, (2 * SLOTS, tokens), 0)
    second = lax.div(slot_at, SLOTS)
    slot_expert = my_expert + second - 2 * my_expert * second
    routes = routes_ref[...]
    hits = jnp.zeros((2 * SLOTS, tokens), F32)
    for k in range(TOP):
        hits += jnp.where(routes[k : k + 1] == slot_expert, 1.0, 0.0)
    row = lax.broadcasted_iota(jnp.int32, (tokens, tokens), 0)
    lane = lax.broadcasted_iota(jnp.int32, (tokens, tokens), 1)
    earlier = (row < lane) & (lax.div(lane, MB_ROWS) == lax.div(row, MB_ROWS))
    rank = jnp.dot(hits.astype(BF16), jnp.where(earlier, 1.0, 0.0).astype(BF16), preferred_element_type=F32)
    slot_rank = lax.rem(slot_at, MOST)
    slot_block = lax.rem(lax.div(slot_at, MOST), MB_DEV)
    fits = (rank == slot_rank.astype(F32)) & (slot_block == lax.div(token, MB_ROWS))
    pick = jnp.where(fits, hits, 0.0)

    load_hidden.wait()
    rows = jnp.dot(pick.astype(BF16), hidden[...], preferred_element_type=F32)
    center = jnp.mean(rows, axis=-1, keepdims=True)
    rows = rows - center
    spread = jnp.mean(jnp.square(rows), axis=-1, keepdims=True)
    rows = rows * lax.rsqrt(spread + EPS) * gain_ref[...].astype(F32)

    def piece(values):
        return jnp.concatenate([values[:, :cols], values[:, cols:]], axis=0).astype(BF16)

    other[...] = piece(rows[SLOTS:])
    x_buf[0] = piece(rows[:SLOTS])

    pl.semaphore_wait(barrier, len(bits))

    def x_copy(src, slot, bit):
        return pltpu.make_async_remote_copy(
            src_ref=src, dst_ref=x_buf.at[slot], send_sem=x_send.at[slot], recv_sem=x_recv.at[slot],
            device_id=peer(bit), device_id_type=MESH)

    sent = [x_copy(other, half, half)]
    sent[-1].start()

    def pass_on(slot):
        for bit in later(slot):
            sent.append(x_copy(x_buf.at[slot], slot ^ bit, bit))
            sent[-1].start()
        sent.append(x_copy(x_buf.at[slot], slot ^ 1, 1))
        sent[-1].start()

    pass_on(0)

    normed = rows.astype(BF16)
    loads[0].wait()
    across = (((1,), (1,)), ((), ()))
    logits = lax.dot_general(normed, router[...], across, preferred_element_type=F32)
    expert_row = lax.broadcasted_iota(jnp.int32, (EXPERTS, tokens), 0)
    chosen = jnp.zeros((EXPERTS, tokens), F32)
    for k in range(TOP):
        chosen += jnp.where(routes[k : k + 1] == expert_row, 1.0, 0.0)
    slot_chosen = lax.dot_general(pick.astype(BF16), chosen.astype(BF16), across, preferred_element_type=F32)
    raised = jnp.where(slot_chosen > 0.5, jnp.exp(logits), 0.0)
    expert_lane = lax.broadcasted_iota(jnp.int32, (2 * SLOTS, EXPERTS), 1)
    top = jnp.sum(jnp.where(expert_lane == slot_expert[:, :EXPERTS], raised, 0.0), axis=-1, keepdims=True)
    total = jnp.sum(raised, axis=-1, keepdims=True)
    filled = jnp.sum(slot_chosen, axis=-1, keepdims=True) > 0.5
    gates = jnp.where(filled, top / jnp.where(filled, total, 1.0), 0.0)
    weighted = jnp.concatenate([pick * gates, jnp.zeros((128 - 2 * SLOTS, tokens), F32)], axis=0).T
    weighted = weighted[:, : 2 * SLOTS]

    for slot in arrival:
        x_copy(other, slot, last_bit(slot)).wait_recv()
        pass_on(slot)
    for slot in range(1, n, 2):
        x_copy(other, slot, 1).wait_recv()

    loads[1].wait()
    loads[2].wait()
    loads[3].wait()

    group = min(n, 16)

    def project(at, carry):
        base = pl.multiple_of(at * group, group)
        x = x_buf[pl.ds(base, group)].reshape(group * 2 * SLOTS, cols)
        w_lo = jnp.concatenate([wg[:cols], wu[:cols]], axis=1)
        w_hi = jnp.concatenate([wg[cols:], wu[cols:]], axis=1)
        lo = jnp.dot(x, w_lo, preferred_element_type=F32).reshape(group, 2 * SLOTS, -1)[:, :SLOTS]
        hi = jnp.dot(x, w_hi, preferred_element_type=F32).reshape(group, 2 * SLOTS, -1)[:, SLOTS:]
        both = (lo + hi).reshape(group * SLOTS, -1)
        unit = both.shape[1] // 2
        gate, up = both[:, :unit], both[:, unit:]
        act = (gate / (1.0 + jnp.exp(-gate)) * up).astype(BF16)
        step = 512
        for c in range(0, cols, step):
            y_lo = jnp.dot(act, wd[:, c : c + step], preferred_element_type=F32)
            y_hi = jnp.dot(act, wd[:, cols + c : cols + c + step], preferred_element_type=F32)
            y = jnp.concatenate(
                [y_lo.reshape(group, SLOTS, step), y_hi.reshape(group, SLOTS, step)], axis=1)
            y_buf[pl.ds(base, group), :, c : c + step] = y.astype(BF16)
        return carry

    if n == group:
        project(0, 0)
    else:
        lax.fori_loop(0, n // group, project, 0)

    def z_copy(slot, bit):
        return pltpu.make_async_remote_copy(
            src_ref=y_buf.at[slot], dst_ref=z_buf.at[slot], send_sem=z_send.at[slot], recv_sem=z_recv.at[slot],
            device_id=peer(bit), device_id_type=MESH)

    back = arrival[::-1]
    for slot in back + [0]:
        z_copy(slot ^ 1, 1).start()

    def summed(slot):
        value = y_buf[slot].astype(F32)
        for bit in [1] + later(slot)[::-1]:
            z_copy(slot ^ bit, bit).wait_recv()
            value += z_buf[slot ^ bit].astype(F32)
        return value

    for slot in back:
        y_buf[slot] = summed(slot).astype(BF16)
        z_copy(slot, last_bit(slot)).start()

    mine = summed(0)
    z_copy(half, half).wait_recv()
    theirs = z_buf[half].astype(F32)
    outs = []
    for part in range(2):
        sums = jnp.concatenate(
            [mine[part * SLOTS : (part + 1) * SLOTS], theirs[part * SLOTS : (part + 1) * SLOTS]], axis=0)
        span = slice(part * cols, (part + 1) * cols)
        mixed = jnp.dot(weighted, sums, preferred_element_type=F32, precision=lax.Precision.HIGHEST)
        out[:, span] = (hidden[:, span].astype(F32) + mixed).astype(BF16)
        outs.append(pltpu.make_async_copy(out.at[:, span], out_hbm.at[:, span], out_sem.at[part]))
        outs[-1].start()

    for copy in sent:
        copy.wait_send()
    for slot in range(1, n):
        z_copy(slot, last_bit(slot)).wait_send()
    for copy in outs:
        copy.wait()


def body(hidden, ln_gain, router, routes, w_gate, w_up, w_down):
    n = lax.axis_size("tok")
    tokens, width = hidden.shape
    units = w_gate.shape[-1]
    piece = (2 * SLOTS, width // 2)
    any_spec = pl.BlockSpec(memory_space=pl.ANY)
    vmem = pl.BlockSpec(memory_space=pltpu.VMEM)
    return pl.pallas_call(
        functools.partial(kernel, n),
        out_shape=jax.ShapeDtypeStruct((tokens, width), BF16),
        in_specs=[any_spec, vmem, any_spec, vmem, any_spec, any_spec, any_spec],
        out_specs=any_spec,
        scratch_shapes=[
            pltpu.VMEM((tokens, width), BF16),
            pltpu.VMEM(router.shape[::-1], BF16),
            pltpu.VMEM((width, units), BF16),
            pltpu.VMEM((width, units), BF16),
            pltpu.VMEM((units, width), BF16),
            pltpu.VMEM((n,) + piece, BF16),
            pltpu.VMEM(piece, BF16),
            pltpu.VMEM((n,) + piece, BF16),
            pltpu.VMEM((n,) + piece, BF16),
            pltpu.VMEM((tokens, width), BF16),
            pltpu.SemaphoreType.DMA((5,)),
            pltpu.SemaphoreType.DMA((2,)),
            pltpu.SemaphoreType.DMA((n,)),
            pltpu.SemaphoreType.DMA((n,)),
            pltpu.SemaphoreType.DMA((n,)),
            pltpu.SemaphoreType.DMA((n,)),
        ],
        compiler_params=pltpu.CompilerParams(
            collective_id=0, has_side_effects=True, vmem_limit_bytes=56 * 1024 * 1024
        ),
        name="expert_exchange",
    )(
        hidden,
        ln_gain.reshape(1, width),
        router.T,
        routes.T,
        w_gate.reshape(width, units),
        w_up.reshape(width, units),
        w_down.reshape(units, width),
    )


def solution(mesh):
    in_specs = (
        P(("group", "tok"), None),
        P(),
        P(),
        P(("group", "tok"), None),
        P("tok", None, None),
        P("tok", None, None),
        P("tok", None, None),
    )
    out_specs = P(("group", "tok"), None)
    return jax.shard_map(body, mesh=mesh, in_specs=in_specs, out_specs=out_specs, check_vma=False)
```

time: 136 us -> 49.6 us (0.36)
  the two profiles are of different devices: /device:TPU:15 before, /device:TPU:0 now
where the time goes in v1:
time: 49.6 us; the launch traced here: 49.4 us
  Pallas kernels  45.3 us (91%)
  local copies, waits for them, and re-layouts  4.02 us (8%)
    pallas_call x1, Pallas kernels, body(): pl.pallas_call(functools.partial(kernel, n), out_shape=jax.ShapeDtypeStru...  45.3 us
    unnamed x1, local copies, waits for them, and re-layouts  2.69 us
    reshape x1, local copies, waits for them, and re-layouts, body(): ln_gain.reshape(1, width)  1.33 us

profile of v1, /device:TPU:0, one launch (start us, length us, event | category | flops | bytes accessed | tf_op | source)
XLA Modules:
  0.0 49.4 jit_solution(14811022505113493868)
XLA Ops:
  0.0 1.3 %reshape.12.gain_ref = bf16[1,6144]{1,0:T(2,128)(2,1)} reshape(bf16[6144]{0:T(1024)(128)(2,1)} %param.8) | data formatting | bytes 24576 | tf_op jit(solution)/shard_map/reshape | solution.py:267
  1.3 45.3 %expert_exchange.1 = bf16[128,6144]{1,0:T(8,128)(2,1)} custom-call(bf16[128,6144]{1,0:T(8,128)(2,1)} %hidden_hbm.1, bf16[1,6144]{1,0:T(2,128)(2,1)} %reshape.12.gain_ref, bf16[16,6144]{1,0:T(8,128)(2,1)} %bitcast.8, s32[4,128]{1,0:T(4,128)} %bitcast.9, bf16[6144,128]{1,0:T(8,128)(2,1)} %bitcast.5, bf16[6144,128]{1,0:T(8,128)(2,1)} %bitcast.6, ...), custom_call_target="tpu_custom_call" | custom-call | tf_op jit(solution)/shard_map/expert_exchange/pallas_call | solution.py:238
  46.7 2.7 %copy.9 = bf16[128,6144]{1,0:T(8,128)(2,1)} copy(bf16[128,6144]{1,0:T(8,128)(2,1)} %expert_exchange.1) | data formatting | bytes 3145728

commit v2 on v1

v2 whole, which is shorter than its diff:
```python
import functools

import jax
import jax.numpy as jnp
from jax import lax
from jax.experimental import pallas as pl
from jax.experimental.pallas import tpu as pltpu
from jax.sharding import PartitionSpec as P

EXPERTS = 16
TOP = 4
EXP_WIN = 2
MB_ROWS = 64
MB_DEV = 2
MOST = 4
SLOTS = MB_DEV * MOST
TILE = 16
SPLIT = TILE // MOST

EPS = 1e-05
MESH = pl.DeviceIdType.MESH
F32 = jnp.float32
BF16 = jnp.bfloat16


def routes_plan(n):
    bits = n.bit_length() - 1
    inner = [1 << b for b in range(1, bits - 1)]
    half = n // 2
    orders = {0: inner[::-1], half: inner}

    def chain(slot):
        return half if slot & half else 0

    def later(slot):
        order = orders[chain(slot)]
        last = -1
        for at, bit in enumerate(order):
            if slot & bit:
                last = at
        return order[last + 1 :]

    def last_bit(slot):
        if slot & 1:
            return 1
        found = half
        for bit in orders[chain(slot)]:
            if slot & bit:
                found = bit
        return found

    evens = [slot for slot in range(n) if not slot & 1]

    def depth(slot):
        return bin(slot).count("1") + (1 if slot & half else 0)

    arrival = sorted([slot for slot in evens if slot], key=lambda slot: (depth(slot), slot & half))
    return later, last_bit, [(slot, depth(slot)) for slot in arrival]


def kernel(n, hidden_hbm, gain_ref, router_hbm, routes_ref, wg_hbm, wu_hbm, wd_hbm, out_hbm,
           hidden, router, wg, wu, wd, x_buf, other, y_buf, z_buf, out,
           in_sem, out_sem, x_send, x_recv, z_send, z_recv):
    later, last_bit, levels = routes_plan(n)
    arrival = [slot for slot, _ in levels]
    half = n // 2
    tokens, width = hidden.shape
    cols = width // SPLIT
    me = lax.axis_index("tok")

    def peer(bit):
        return {"tok": me + bit * (1 - 2 * lax.rem(lax.div(me, bit), 2))}

    load_hidden = pltpu.make_async_copy(hidden_hbm, hidden, in_sem.at[0])
    load_hidden.start()
    loads = [
        pltpu.make_async_copy(src, dst, in_sem.at[1 + at])
        for at, (src, dst) in enumerate(((router_hbm, router), (wg_hbm, wg), (wu_hbm, wu), (wd_hbm, wd)))
    ]
    for load in loads:
        load.start()

    barrier = pltpu.get_barrier_semaphore()
    bits = [1 << b for b in range(n.bit_length() - 1)]
    for bit in bits:
        pl.semaphore_signal(barrier, inc=1, device_id=peer(bit), device_id_type=MESH)

    my_expert = lax.div(me, half)
    token = lax.broadcasted_iota(jnp.int32, (2 * SLOTS, tokens), 1)
    slot_at = lax.broadcasted_iota(jnp.int32, (2 * SLOTS, tokens), 0)
    second = lax.rem(lax.div(slot_at, MOST), 2)
    slot_expert = my_expert + second - 2 * my_expert * second
    routes = routes_ref[...]
    hits = jnp.zeros((2 * SLOTS, tokens), F32)
    for k in range(TOP):
        hits += jnp.where(routes[k : k + 1] == slot_expert, 1.0, 0.0)
    row = lax.broadcasted_iota(jnp.int32, (tokens, tokens), 0)
    lane = lax.broadcasted_iota(jnp.int32, (tokens, tokens), 1)
    earlier = (row < lane) & (lax.div(lane, MB_ROWS) == lax.div(row, MB_ROWS))
    rank = jnp.dot(hits.astype(BF16), jnp.where(earlier, 1.0, 0.0).astype(BF16), preferred_element_type=F32)
    slot_rank = lax.rem(slot_at, MOST)
    slot_block = lax.div(slot_at, SLOTS)
    fits = (rank == slot_rank.astype(F32)) & (slot_block == lax.div(token, MB_ROWS))
    pick = jnp.where(fits, hits, 0.0)

    load_hidden.wait()
    rows = jnp.dot(pick.astype(BF16), hidden[...], preferred_element_type=F32)
    center = jnp.mean(rows, axis=-1, keepdims=True)
    rows = rows - center
    spread = jnp.mean(jnp.square(rows), axis=-1, keepdims=True)
    rows = rows * lax.rsqrt(spread + EPS) * gain_ref[...].astype(F32).reshape(1, width)

    normed = rows.astype(BF16)

    pieces = MB_DEV * EXP_WIN
    spread_row = lax.broadcasted_iota(jnp.int32, (pieces * TILE, SPLIT * TILE), 0)
    spread_col = lax.broadcasted_iota(jnp.int32, (pieces * TILE, SPLIT * TILE), 1)
    same_slot = (lax.div(spread_row, TILE) == lax.div(lax.rem(spread_col, TILE), MOST)) & (
        lax.rem(spread_row, MOST) == lax.rem(spread_col, MOST))
    same_part = lax.div(lax.rem(spread_row, TILE), MOST) == lax.div(spread_col, TILE)
    spread_out = jnp.where(same_slot & same_part, 1.0, 0.0).astype(BF16)
    stacked = jnp.concatenate([normed[:, part * cols : (part + 1) * cols] for part in range(SPLIT)], axis=0)
    cut = jnp.dot(spread_out, stacked, preferred_element_type=F32).astype(BF16)
    for mb in range(MB_DEV):
        at = mb * 2 * TILE
        x_buf[mb, 0] = cut[at : at + TILE]
        other[mb] = cut[at + TILE : at + 2 * TILE]

    pl.semaphore_wait(barrier, len(bits))

    def x_copy(mb, src, slot, bit):
        return pltpu.make_async_remote_copy(
            src_ref=src, dst_ref=x_buf.at[mb, slot], send_sem=x_send.at[mb, slot], recv_sem=x_recv.at[mb, slot],
            device_id=peer(bit), device_id_type=MESH)

    sent = []

    def pass_on(mb, slot):
        for bit in later(slot) + [1]:
            sent.append(x_copy(mb, x_buf.at[mb, slot], slot ^ bit, bit))
            sent[-1].start()

    for mb in range(MB_DEV):
        sent.append(x_copy(mb, other.at[mb], half, half))
        sent[-1].start()
        pass_on(mb, 0)

    loads[0].wait()
    across = (((1,), (1,)), ((), ()))
    logits = lax.dot_general(normed, router[...], across, preferred_element_type=F32)
    expert_row = lax.broadcasted_iota(jnp.int32, (EXPERTS, tokens), 0)
    chosen = jnp.zeros((EXPERTS, tokens), F32)
    for k in range(TOP):
        chosen += jnp.where(routes[k : k + 1] == expert_row, 1.0, 0.0)
    slot_chosen = lax.dot_general(pick.astype(BF16), chosen.astype(BF16), across, preferred_element_type=F32)
    raised = jnp.where(slot_chosen > 0.5, jnp.exp(logits), 0.0)
    expert_lane = lax.broadcasted_iota(jnp.int32, (2 * SLOTS, EXPERTS), 1)
    top = jnp.sum(jnp.where(expert_lane == slot_expert[:, :EXPERTS], raised, 0.0), axis=-1, keepdims=True)
    total = jnp.sum(raised, axis=-1, keepdims=True)
    filled = jnp.sum(slot_chosen, axis=-1, keepdims=True) > 0.5
    gates = jnp.where(filled, top / jnp.where(filled, total, 1.0), 0.0)
    weighted = pick * gates
    weights = []
    lane_part = lax.rem(lax.div(lax.broadcasted_iota(jnp.int32, (MB_ROWS, 128), 1), MOST), SPLIT)
    high = weighted.astype(BF16).astype(F32)
    low = weighted - high
    for mb in range(MB_DEV):
        def four(values, e):
            at = mb * SLOTS + e * MOST
            return [values[at : at + MOST]] * SPLIT
        tall = four(high, 0) + four(high, 1) + four(low, 0) + four(low, 1) + four(high, 0)
        tall = jnp.concatenate(tall + [jnp.zeros((128 - 5 * TILE, tokens), F32)], axis=0).T
        tall = tall[mb * MB_ROWS : (mb + 1) * MB_ROWS]
        weights.append([jnp.where(lane_part == part, tall, 0.0).astype(BF16) for part in range(SPLIT)])

    def arrive(mb, slot):
        x_copy(mb, other.at[mb], slot, last_bit(slot)).wait_recv()
        if not slot & 1:
            pass_on(mb, slot)

    group = min(n, 16)
    tall_rows = group * TILE
    part_of = lax.rem(lax.div(lax.broadcasted_iota(jnp.int32, (tall_rows, 1), 0), MOST), SPLIT)
    one = lax.broadcasted_iota(jnp.int32, (tall_rows, tall_rows), 0)
    two = lax.broadcasted_iota(jnp.int32, (tall_rows, tall_rows), 1)
    same = (lax.div(one, TILE) == lax.div(two, TILE)) & (lax.rem(one, MOST) == lax.rem(two, MOST))
    gather_parts = jnp.where(same, 1.0, 0.0)

    def project(mb):
        def step_of(at, carry):
            base = pl.multiple_of(at * group, group)
            x = x_buf[mb, pl.ds(base, group)].reshape(tall_rows, cols)
            both = jnp.zeros((tall_rows, 2 * wg.shape[1]), F32)
            for part in range(SPLIT):
                span = slice(part * cols, (part + 1) * cols)
                w = jnp.concatenate([wg[span], wu[span]], axis=1)
                both += jnp.where(part_of == part, jnp.dot(x, w, preferred_element_type=F32), 0.0)
            both = jnp.dot(gather_parts, both, preferred_element_type=F32, precision=lax.Precision.HIGHEST)
            unit = both.shape[1] // 2
            gate, up = both[:, :unit], both[:, unit:]
            act = gate / (1.0 + jnp.exp(-gate)) * up
            act = jnp.concatenate(
                [jnp.where(part_of == part, act, 0.0).astype(BF16) for part in range(SPLIT)], axis=1)
            step = 512
            for c in range(0, cols, step):
                w = jnp.concatenate(
                    [wd[:, part * cols + c : part * cols + c + step] for part in range(SPLIT)], axis=0)
                y = jnp.dot(act, w, preferred_element_type=F32)
                y_buf[mb, pl.ds(base, group), :, c : c + step] = y.reshape(group, TILE, step).astype(BF16)
            return carry

        if n == group:
            step_of(0, 0)
        else:
            lax.fori_loop(0, n // group, step_of, 0)

    def z_copy(mb, slot, bit):
        return pltpu.make_async_remote_copy(
            src_ref=y_buf.at[mb, slot], dst_ref=z_buf.at[mb, slot],
            send_sem=z_send.at[mb, slot], recv_sem=z_recv.at[mb, slot],
            device_id=peer(bit), device_id_type=MESH)

    back = levels[::-1]

    def start_back(mb):
        for slot in arrival[::-1] + [0]:
            z_copy(mb, slot ^ 1, 1).start()

    def summed(mb, slot):
        value = y_buf[mb, slot].astype(F32)
        for bit in [1] + later(slot)[::-1]:
            z_copy(mb, slot ^ bit, bit).wait_recv()
            value += z_buf[mb, slot ^ bit].astype(F32)
        return value

    def send_back(mb, slot):
        y_buf[mb, slot] = summed(mb, slot).astype(BF16)
        z_copy(mb, slot, last_bit(slot)).start()

    outs = []

    def finish(mb):
        mine = summed(mb, 0)
        z_copy(mb, half, half).wait_recv()
        theirs = z_buf[mb, half]
        mine_high = mine.astype(BF16)
        mine_low = (mine - mine_high.astype(F32)).astype(BF16)
        sums = jnp.concatenate(
            [mine_high, theirs, mine_high, theirs, mine_low, jnp.zeros((128 - 5 * TILE, cols), BF16)], axis=0)
        span = slice(mb * MB_ROWS, (mb + 1) * MB_ROWS)
        mixed = jnp.dot(jnp.concatenate(weights[mb], axis=0), sums, preferred_element_type=F32)
        for part in range(SPLIT):
            at = slice(part * cols, (part + 1) * cols)
            term = mixed[part * MB_ROWS : (part + 1) * MB_ROWS]
            out[span, at] = (hidden[span, at].astype(F32) + term).astype(BF16)
        outs.append(pltpu.make_async_copy(out.at[span], out_hbm.at[span], out_sem.at[mb]))
        outs[-1].start()

    deepest = max(level for _, level in levels)
    for level in range(1, deepest + 2):
        for mb in range(MB_DEV):
            for slot, at in levels:
                if at == level - mb:
                    arrive(mb, slot)
        if level == deepest:
            for slot in range(1, n, 2):
                arrive(0, slot)
            for load in loads[1:]:
                load.wait()
            project(0)
            start_back(0)
    first = [slot for slot, at in back if at == deepest]
    for slot in first:
        send_back(0, slot)
    for slot in range(1, n, 2):
        arrive(1, slot)
    project(1)
    start_back(1)
    for level in range(deepest - 1, -1, -1):
        for mb in range(MB_DEV):
            for slot, at in back:
                if at == level + mb:
                    send_back(mb, slot)
        if level == 0:
            for mb in range(MB_DEV):
                finish(mb)

    for copy in sent:
        copy.wait_send()
    for mb in range(MB_DEV):
        for slot in range(1, n):
            z_copy(mb, slot, last_bit(slot)).wait_send()
    for copy in outs:
        copy.wait()


def body(hidden, ln_gain, router, routes, w_gate, w_up, w_down):
    n = lax.axis_size("tok")
    tokens, width = hidden.shape
    units = w_gate.shape[-1]
    piece = (TILE, width // SPLIT)
    any_spec = pl.BlockSpec(memory_space=pl.ANY)
    vmem = pl.BlockSpec(memory_space=pltpu.VMEM)
    return pl.pallas_call(
        functools.partial(kernel, n),
        out_shape=jax.ShapeDtypeStruct((tokens, width), BF16),
        in_specs=[any_spec, vmem, any_spec, vmem, any_spec, any_spec, any_spec],
        out_specs=any_spec,
        scratch_shapes=[
            pltpu.VMEM((tokens, width), BF16),
            pltpu.VMEM(router.shape[::-1], BF16),
            pltpu.VMEM((width, units), BF16),
            pltpu.VMEM((width, units), BF16),
            pltpu.VMEM((units, width), BF16),
            pltpu.VMEM((MB_DEV, n) + piece, BF16),
            pltpu.VMEM((MB_DEV,) + piece, BF16),
            pltpu.VMEM((MB_DEV, n) + piece, BF16),
            pltpu.VMEM((MB_DEV, n) + piece, BF16),
            pltpu.VMEM((tokens, width), BF16),
            pltpu.SemaphoreType.DMA((5,)),
            pltpu.SemaphoreType.DMA((2,)),
            pltpu.SemaphoreType.DMA((MB_DEV, n)),
            pltpu.SemaphoreType.DMA((MB_DEV, n)),
            pltpu.SemaphoreType.DMA((MB_DEV, n)),
            pltpu.SemaphoreType.DMA((MB_DEV, n)),
        ],
        compiler_params=pltpu.CompilerParams(
            collective_id=0, has_side_effects=True, vmem_limit_bytes=56 * 1024 * 1024
        ),
        name="expert_exchange",
    )(
        hidden,
        ln_gain,
        router.T,
        routes.T,
        w_gate.reshape(width, units),
        w_up.reshape(width, units),
        w_down.reshape(units, width),
    )


def solution(mesh):
    in_specs = (
        P(("group", "tok"), None),
        P(),
        P(),
        P(("group", "tok"), None),
        P("tok", None, None),
        P("tok", None, None),
        P("tok", None, None),
    )
    out_specs = P(("group", "tok"), None)
    return jax.shard_map(body, mesh=mesh, in_specs=in_specs, out_specs=out_specs, check_vma=False)
```

time: 49.6 us -> 46 us (0.927)
  Pallas kernels: 45.3 us -> 43.1 us
  local copies, waits for them, and re-layouts: 4.02 us -> 2.69 us
    pallas_call x1, Pallas kernels: 45.3 us -> 43.1 us  [body(): pl.pallas_call(functools.partial(kernel, n), out_shape=jax.ShapeDtypeStru...]
    reshape x1 -> x0, local copies, waits for them, and re-layouts: 1.33 us -> none  [body(): ln_gain.reshape(1, width)]
where the time goes in v2:
time: 46 us; the launch traced here: 45.8 us
  Pallas kernels  43.1 us (94%)
  local copies, waits for them, and re-layouts  2.69 us (6%)
    pallas_call x1, Pallas kernels, body(): pl.pallas_call(functools.partial(kernel, n), out_shape=jax.ShapeDtypeStru...  43.1 us
    unnamed x1, local copies, waits for them, and re-layouts  2.69 us

profile of v2, /device:TPU:0, one launch (start us, length us, event | category | flops | bytes accessed | tf_op | source)
XLA Modules:
  0.0 45.8 jit_solution(4816679005173145421)
XLA Ops:
  0.0 43.1 %expert_exchange.1 = bf16[128,6144]{1,0:T(8,128)(2,1)} custom-call(bf16[128,6144]{1,0:T(8,128)(2,1)} %hidden_hbm.1, bf16[6144]{0:T(1024)(128)(2,1)} %gain_ref.1, bf16[16,6144]{1,0:T(8,128)(2,1)} %bitcast.8, s32[4,128]{1,0:T(4,128)} %bitcast.9, bf16[6144,128]{1,0:T(8,128)(2,1)} %bitcast.5, bf16[6144,128]{1,0:T(8,128)(2,1)} %bitcast.6, bf16[128,6144]{1,0:T(8,128)(2,1)} %bitcast.7), custom_call_target="tpu_custom_call" | custom-call | tf_op jit(solution)/shard_map/expert_exchange/pallas_call | solution.py:304
  43.1 2.7 %copy.9 = bf16[128,6144]{1,0:T(8,128)(2,1)} copy(bf16[128,6144]{1,0:T(8,128)(2,1)} %expert_exchange.1) | data formatting | bytes 3145728

commit v3 on v2

--- a/solution.py
+++ b/solution.py
@@ -143,6 +143,7 @@
     for mb in range(MB_DEV):
         sent.append(x_copy(mb, other.at[mb], half, half))
         sent[-1].start()
+    for mb in range(MB_DEV):
         pass_on(mb, 0)
 
     loads[0].wait()
@@ -276,10 +277,12 @@
         arrive(1, slot)
     project(1)
     start_back(1)
+    for slot in first:
+        send_back(1, slot)
     for level in range(deepest - 1, -1, -1):
         for mb in range(MB_DEV):
             for slot, at in back:
-                if at == level + mb:
+                if at == level:
                     send_back(mb, slot)
         if level == 0:
             for mb in range(MB_DEV):

time: 46 us -> 46 us (level)
  no operation moved by 1% of the time
where the time goes in v3:
time: 46 us; the launch traced here: 45.8 us
  Pallas kernels  43.1 us (94%)
  local copies, waits for them, and re-layouts  2.69 us (6%)
    pallas_call x1, Pallas kernels, body(): pl.pallas_call(functools.partial(kernel, n), out_shape=jax.ShapeDtypeStru...  43.1 us
    unnamed x1, local copies, waits for them, and re-layouts  2.69 us

profile of v3, /device:TPU:0, one launch (start us, length us, event | category | flops | bytes accessed | tf_op | source)
XLA Modules:
  0.0 45.8 jit_solution(6866256600039983807)
XLA Ops:
  0.0 43.1 %expert_exchange.1 = bf16[128,6144]{1,0:T(8,128)(2,1)} custom-call(bf16[128,6144]{1,0:T(8,128)(2,1)} %hidden_hbm.1, bf16[6144]{0:T(1024)(128)(2,1)} %gain_ref.1, bf16[16,6144]{1,0:T(8,128)(2,1)} %bitcast.8, s32[4,128]{1,0:T(4,128)} %bitcast.9, bf16[6144,128]{1,0:T(8,128)(2,1)} %bitcast.5, bf16[6144,128]{1,0:T(8,128)(2,1)} %bitcast.6, bf16[128,6144]{1,0:T(8,128)(2,1)} %bitcast.7), custom_call_target="tpu_custom_call" | custom-call | tf_op jit(solution)/shard_map/expert_exchange/pallas_call | solution.py:307
  43.1 2.7 %copy.9 = bf16[128,6144]{1,0:T(8,128)(2,1)} copy(bf16[128,6144]{1,0:T(8,128)(2,1)} %expert_exchange.1) | data formatting | bytes 3145728
